TPU v7x, 256 devices: a whole 4x4x8 slice. The times are simulated.
256 devices in a mesh: frame: 64 (over z, y, x_lo), row: 4 (over x_hi, core).
Axes of the slice: x: 4 (x_hi: 2, x_lo: 2; x = x_hi * 2 + x_lo), y: 4, z: 8, core: 2. Of those that a mesh axis runs over, the one named last changes fastest.
Arguments:
- video: bfloat16 [64, 512, 1152], P('frame', 'row'), may hold values from -6 to 6
- modulation: float32 [2, 6, 1152], replicated, may hold values from -3 to 3
- query_key_value_weight: bfloat16 [2, 1152, 3, 1152], P(None, 'frame', None, 'row'), may hold values from -8 to 8
- attention_output_weight: bfloat16 [2, 1152, 1152], P(None, 'row', 'frame'), may hold values from -0.1875 to 0.1875
- feed_forward_up_weight: bfloat16 [2, 1152, 4608], P(None, 'frame', 'row'), may hold values from -0.1875 to 0.1875
- feed_forward_down_weight: bfloat16 [2, 4608, 1152], P(None, 'row', 'frame'), may hold values from -0.09375 to 0.09375
Outputs:
- denoised: bfloat16 [64, 512, 1152], P('frame', 'row')
All inputs are finite; a program needn't handle non-finite values.
Results may differ from a plain program's by a relative error of at most 0.013.
Values may be sent and summed in bfloat16 or wider, within the bound.
No kernel may reach another device: no remote copies, remote signals or barrier semaphores. Data moves between devices by JAX's collectives and lax.ppermute only.
A program may use at most 64 MiB of HBM per device.

v0:
```python
import jax
import jax.numpy as jnp
from jax import lax
from jax.sharding import PartitionSpec as P

HEADS = 16


epsilon = 1e-06


def normalize(token_sequence, shift, scale):
    values = token_sequence.astype(jnp.float32)
    center = values - jnp.mean(values, axis=-1, keepdims=True)
    spread = jnp.mean(center * center, axis=-1, keepdims=True)
    return (center * lax.rsqrt(spread + epsilon) * (1.0 + scale) + shift).astype(jnp.bfloat16)


def attend(query_part, key_part, value_part):
    head_size = query_part.shape[-1]
    scores = jnp.einsum(
        "blhd,bmhd->bhlm", query_part, key_part, preferred_element_type=jnp.float32
    ) * head_size ** (-0.5)
    scores = scores - jnp.max(scores, axis=-1, keepdims=True)
    raised = jnp.exp(scores)
    probs = (raised / jnp.sum(raised, axis=-1, keepdims=True)).astype(jnp.bfloat16)
    return jnp.einsum(
        "bhlm,bmhd->blhd", probs, value_part, preferred_element_type=jnp.float32
    ).astype(jnp.bfloat16)


def gather_rows(normed):
    return lax.all_gather(normed, "row", axis=0, tiled=True)


def project_in(normed_all, weight_local):
    flat = weight_local.reshape(weight_local.shape[0], -1)
    whole = lax.all_gather(flat, "frame", axis=0, tiled=True)
    return jnp.dot(normed_all, whole, preferred_element_type=jnp.float32)


def project_out(parts, weight_local):
    full_weight = lax.all_gather(weight_local, "frame", axis=1, tiled=True)
    return lax.psum_scatter(
        jnp.dot(parts, full_weight, preferred_element_type=jnp.float32),
        "row",
        scatter_dimension=0,
        tiled=True,
    )


def project_attention(mixed, weight_local):
    return project_out(mixed, weight_local)


def feed_forward(token_sequence, modulation, leading_block, trailing_block):
    normed = normalize(token_sequence, modulation[3], modulation[4])
    hidden = project_in(gather_rows(normed), leading_block)
    activated = jax.nn.gelu(hidden, approximate=True).astype(jnp.bfloat16)
    update = project_out(activated, trailing_block)
    return (token_sequence.astype(jnp.float32) + modulation[5] * update).astype(jnp.bfloat16)


def on_device(
    video,
    modulation,
    query_key_value_weight,
    attention_output_weight,
    feed_forward_up_weight,
    feed_forward_down_weight,
):
    token_sequence = video[0]
    own_rows, width = token_sequence.shape
    head_size = width // HEADS
    ranks = lax.axis_size("row")
    heads_local = HEADS // ranks
    local_width = heads_local * head_size
    frames = lax.axis_size("frame")
    spatial_mod = modulation[0]
    normed = normalize(token_sequence, spatial_mod[0], spatial_mod[1])
    packed = project_in(gather_rows(normed), query_key_value_weight[0]).astype(jnp.bfloat16)
    triple = packed.reshape(1, -1, 3, heads_local, head_size)
    mixed = attend(triple[:, :, 0], triple[:, :, 1], triple[:, :, 2]).reshape(-1, local_width)
    update = project_attention(mixed, attention_output_weight[0])
    token_sequence = (token_sequence.astype(jnp.float32) + spatial_mod[2] * update).astype(
        jnp.bfloat16
    )
    token_sequence = feed_forward(
        token_sequence, spatial_mod, feed_forward_up_weight[0], feed_forward_down_weight[0]
    )
    temporal_mod = modulation[1]
    normed = normalize(token_sequence, temporal_mod[0], temporal_mod[1])
    packed = project_in(gather_rows(normed), query_key_value_weight[1]).astype(jnp.bfloat16)
    moved = lax.all_to_all(
        packed.reshape(1, packed.shape[0], packed.shape[1]),
        "frame",
        split_axis=1,
        concat_axis=0,
        tiled=True,
    )
    triple = jnp.swapaxes(moved.reshape(frames, -1, 3, heads_local, head_size), 0, 1)
    mixed = attend(triple[:, :, 0], triple[:, :, 1], triple[:, :, 2])
    mixed = jnp.swapaxes(mixed, 0, 1).reshape(frames, -1, local_width)
    returned = lax.all_to_all(mixed, "frame", split_axis=0, concat_axis=1, tiled=True)
    update = project_attention(returned.reshape(-1, local_width), attention_output_weight[1])
    token_sequence = (token_sequence.astype(jnp.float32) + temporal_mod[2] * update).astype(
        jnp.bfloat16
    )
    token_sequence = feed_forward(
        token_sequence, temporal_mod, feed_forward_up_weight[1], feed_forward_down_weight[1]
    )
    return token_sequence.reshape(1, own_rows, width)


def solution(mesh):
    in_specs = (
        P("frame", "row", None),
        P(),
        P(None, "frame", None, "row"),
        P(None, "row", "frame"),
        P(None, "frame", "row"),
        P(None, "row", "frame"),
    )
    out_specs = P("frame", "row", None)
    return jax.shard_map(
        on_device, mesh=mesh, in_specs=in_specs, out_specs=out_specs, check_vma=False
    )
```

profile of v0, /device:TPU:2, one launch (start us, length us, event | category | flops | bytes accessed | tf_op | source)
XLA Modules:
  0.0 2392.5 jit_solution(10701038894466408068)
XLA Ops:
  15.0 165.5 %all-gather = bf16[1,288,1152]{1,0,2:T(2,128)(2,1)S(1)} all-gather(bf16[1,288,18]{1,0,2:T(2,128)(2,1)S(1)} %get-tuple-element.29), channel_id=2, replica_groups=mesh['frame'=64,'row'=4] {'frame'}, dimensions={2}, use_global_device_ids=true | all-gather | bytes 673920 | tf_op jit(solution)/shard_map/all_gather | solution.py:43
  184.3 128.4 %all-gather.35.cloned.1.call-done = bf16[64,18,864]{2,1,0:T(8,128)(2,1)} async-done(((bf16[1,18,864]{2,1,0:T(8,128)(2,1)}), bf16[64,18,864]{2,1,0:T(8,128)(2,1)}) %all-gather.35.cloned.1.call-update) | async-done | bytes 1990672 | tf_op jit(solution)/shard_map/all_gather | solution.py:38
  317.1 19.7 all-gather.19.cloned.1.call-done
  350.3 42.9 %reduce-scatter.5.cloned.1.call-done = f32[128,1152]{1,0:T(8,128)} async-done(((f32[512,1152]{1,0:T(8,128)}), f32[128,1152]{1,0:T(8,128)}) %reduce-scatter.5.cloned.1.call-update) | async-done | bytes 589840 | tf_op jit(solution)/shard_map/reduce_scatter | solution.py:44
  395.7 305.3 %all-gather.29.cloned.1.call-done = bf16[1,1152,1152]{1,0,2:T(2,128)(2,1)} async-done(((bf16[1,1152,18]{1,0,2:T(2,128)(2,1)}), bf16[1,1152,1152]{1,0,2:T(2,128)(2,1)}) %all-gather.29.cloned.1.call-update) | async-done | bytes 2654224 | tf_op jit(solution)/shard_map/all_gather | solution.py:43
  701.1 10.9 copy.23
  711.9 295.3 %all-gather.27.cloned.1.call-done = bf16[1,1152,1152]{2,0,1:T(2,128)(2,1)} async-done(((bf16[1,18,1152]{2,0,1:T(2,128)(2,1)}), bf16[1,1152,1152]{2,0,1:T(2,128)(2,1)}) %all-gather.27.cloned.1.call-update) | async-done | bytes 2654224 | tf_op jit(solution)/shard_map/all_gather | solution.py:38
  1007.2 24.1 %all-gather.21.cloned.1.call-done = bf16[512,1152]{1,0:T(8,128)(2,1)} async-done(((bf16[128,1152]{1,0:T(8,128)(2,1)}), bf16[512,1152]{1,0:T(8,128)(2,1)}) %all-gather.21.cloned.1.call-update) | async-done | bytes 1179664 | tf_op jit(solution)/shard_map/all_gather | solution.py:33
  1031.3 7.9 fusion.13
  1040.3 43.7 %reduce-scatter.7.cloned.1.call-done = f32[128,1152]{1,0:T(8,128)} async-done(((f32[512,1152]{1,0:T(8,128)}), f32[128,1152]{1,0:T(8,128)}) %reduce-scatter.7.cloned.1.call-update) | async-done | bytes 589840 | tf_op jit(solution)/shard_map/reduce_scatter | solution.py:44
  1086.5 300.4 %all-gather.37.cloned.1.call-done = bf16[64,18,864]{2,1,0:T(8,128)(2,1)} async-done(((bf16[1,18,864]{2,1,0:T(8,128)(2,1)}), bf16[64,18,864]{2,1,0:T(8,128)(2,1)}) %all-gather.37.cloned.1.call-update) | async-done | bytes 1990672 | tf_op jit(solution)/shard_map/all_gather | solution.py:38
  1390.0 20.5 all-gather.23.cloned.1.call-done
  1416.3 6.5 reduce.35
  1423.9 36.3 %all_to_all.8 = bf16[64,2,3456]{2,1,0:T(2,128)(2,1)S(1)} all-to-all(bf16[64,2,3456]{2,1,0:T(2,128)(2,1)S(1)} %reshape.201), channel_id=1, replica_groups=mesh['frame'=64,'row'=4] {'frame'}, dimensions={0} | all-to-all | bytes 1769472 | tf_op jit(solution)/shard_map/all_to_all | solution.py:94
  1462.0 5.2 bitcast_reduce_fusion
  1472.2 6.8 all-to-all-start.1
  1479.1 165.2 %all-gather.3 = bf16[1,288,1152]{1,0,2:T(2,128)(2,1)S(1)} all-gather(bf16[1,288,18]{1,0,2:T(2,128)(2,1)S(1)} %get-tuple-element.30), channel_id=5, replica_groups=mesh['frame'=64,'row'=4] {'frame'}, dimensions={2}, use_global_device_ids=true | all-gather | bytes 673920 | tf_op jit(solution)/shard_map/all_gather | solution.py:43
  1651.6 41.4 %reduce-scatter.9.cloned.1.call-done = f32[128,1152]{1,0:T(8,128)} async-done(((f32[512,1152]{1,0:T(8,128)}), f32[128,1152]{1,0:T(8,128)}) %reduce-scatter.9.cloned.1.call-update) | async-done | bytes 589840 | tf_op jit(solution)/shard_map/reduce_scatter | solution.py:44
  1695.8 305.2 %all-gather.33.cloned.1.call-done = bf16[1,1152,1152]{1,0,2:T(2,128)(2,1)} async-done(((bf16[1,1152,18]{1,0,2:T(2,128)(2,1)}), bf16[1,1152,1152]{1,0,2:T(2,128)(2,1)}) %all-gather.33.cloned.1.call-update) | async-done | bytes 2654224 | tf_op jit(solution)/shard_map/all_gather | solution.py:43
  2001.0 10.9 copy.29
  2011.9 295.2 %all-gather.31.cloned.1.call-done = bf16[1,1152,1152]{2,0,1:T(2,128)(2,1)} async-done(((bf16[1,18,1152]{2,0,1:T(2,128)(2,1)}), bf16[1,1152,1152]{2,0,1:T(2,128)(2,1)}) %all-gather.31.cloned.1.call-update) | async-done | bytes 2654224 | tf_op jit(solution)/shard_map/all_gather | solution.py:38
  2307.1 23.9 %all-gather.25.cloned.1.call-done = bf16[512,1152]{1,0:T(8,128)(2,1)} async-done(((bf16[128,1152]{1,0:T(8,128)(2,1)}), bf16[512,1152]{1,0:T(8,128)(2,1)}) %all-gather.25.cloned.1.call-update) | async-done | bytes 1179664 | tf_op jit(solution)/shard_map/all_gather | solution.py:33
  2331.0 7.9 fusion.11
  2339.0 44.7 %reduce-scatter.11.cloned.1.call-done = f32[128,1152]{1,0:T(8,128)} async-done(((f32[512,1152]{1,0:T(8,128)}), f32[128,1152]{1,0:T(8,128)}) %reduce-scatter.11.cloned.1.call-update) | async-done | bytes 589840 | tf_op jit(solution)/shard_map/reduce_scatter | solution.py:44
  (84 shorter events, 64.8 us)
Async XLA Ops:
  6.5 306.1 %all-gather.35.cloned.1.call-start = ((), (), s32[]{:S(2)}) async-start(), calls=%async_computation.18 | async-start | bytes 2795520 | tf_op jit(solution)/shard_map/all_gather | solution.py:38
  8.7 328.0 %all-gather.19.cloned.1.call-start = ((), (), s32[]{:S(2)}) async-start(), calls=%async_computation.6 | async-start | bytes 1474560 | tf_op jit(solution)/shard_map/all_gather | solution.py:33
  14.1 379.2 %reduce-scatter.5.cloned.1.call-start = ((), (), s32[]{:S(2)}) async-start(), calls=%async_computation.7 | async-start | bytes 2949120 | tf_op jit(solution)/shard_map/reduce_scatter | solution.py:44
  346.2 2.4 copy-start.1
  346.2 3.3 copy-start.2
  348.5 44.7 %copy-start = (bf16[1,128,1152]{2,1,0:T(8,128)(2,1)S(1)}, bf16[1,128,1152]{2,1,0:T(8,128)(2,1)}, u32[]{:S(2)}) copy-start(bf16[1,128,1152]{2,1,0:T(8,128)(2,1)} %param.6) | copy-start | bytes 884740
  348.5 352.6 %all-gather.29.cloned.1.call-start = ((), (), s32[]{:S(2)}) async-start(), calls=%async_computation.15 | async-start | bytes 5391360 | tf_op jit(solution)/shard_map/all_gather | solution.py:43
  349.4 657.8 %all-gather.27.cloned.1.call-start = ((), (), s32[]{:S(2)}) async-start(), calls=%async_computation.14 | async-start | bytes 5391360 | tf_op jit(solution)/shard_map/all_gather | solution.py:38
  350.3 681.1 %all-gather.21.cloned.1.call-start = ((), (), s32[]{:S(2)}) async-start(), calls=%async_computation.8 | async-start | bytes 1474560 | tf_op jit(solution)/shard_map/all_gather | solution.py:33
  395.7 688.3 %reduce-scatter.7.cloned.1.call-start = ((), (), s32[]{:S(2)}) async-start(), calls=%async_computation.9 | async-start | bytes 2949120 | tf_op jit(solution)/shard_map/reduce_scatter | solution.py:44
  1039.2 347.6 %all-gather.37.cloned.1.call-start = ((), (), s32[]{:S(2)}) async-start(), calls=%async_computation.19 | async-start | bytes 2795520 | tf_op jit(solution)/shard_map/all_gather | solution.py:38
  1040.0 370.4 %all-gather.23.cloned.1.call-start = ((), (), s32[]{:S(2)}) async-start(), calls=%async_computation.10 | async-start | bytes 1474560 | tf_op jit(solution)/shard_map/all_gather | solution.py:33
  1472.2 175.9 %all-to-all-start.1 = ((bf16[64,8,288]{2,1,0:T(8,128)(2,1)}), bf16[64,8,288]{2,1,0:T(8,128)(2,1)S(1)}, u32[]{:S(2)}, u32[]{:S(2)}) async-start(bf16[64,8,288]{2,1,0:T(8,128)(2,1)} %reshape.171), calls=%async_computation.3 | async-start | bytes 786432 | tf_op jit(solution)/shard_map/all_to_all | solution.py:104
  1479.0 214.0 %reduce-scatter.9.cloned.1.call-start = ((), (), s32[]{:S(2)}) async-start(), calls=%async_computation.11 | async-start | bytes 2949120 | tf_op jit(solution)/shard_map/reduce_scatter | solution.py:44
  1650.3 350.7 %all-gather.33.cloned.1.call-start = ((), (), s32[]{:S(2)}) async-start(), calls=%async_computation.17 | async-start | bytes 5391360 | tf_op jit(solution)/shard_map/all_gather | solution.py:43
  1651.0 656.1 %all-gather.31.cloned.1.call-start = ((), (), s32[]{:S(2)}) async-start(), calls=%async_computation.16 | async-start | bytes 5391360 | tf_op jit(solution)/shard_map/all_gather | solution.py:38
  1651.6 679.4 %all-gather.25.cloned.1.call-start = ((), (), s32[]{:S(2)}) async-start(), calls=%async_computation.12 | async-start | bytes 1474560 | tf_op jit(solution)/shard_map/all_gather | solution.py:33
  1695.5 688.2 %reduce-scatter.11.cloned.1.call-start = ((), (), s32[]{:S(2)}) async-start(), calls=%async_computation.13 | async-start | bytes 2949120 | tf_op jit(solution)/shard_map/reduce_scatter | solution.py:44
Sparse Core Ops, SparseCore 0:
  9.2 303.4 all-gather.34
  314.5 22.1 all-gather.18
  348.6 44.5 reduce-scatter.4
  395.0 306.0 all-gather.28
  702.8 304.3 all-gather.26
  1009.0 22.2 all-gather.20
  1039.4 44.5 reduce-scatter.6
  1085.8 301.0 all-gather.36
  1388.7 21.7 all-gather.22
  1650.4 42.5 reduce-scatter.8
  1694.9 306.0 all-gather.32
  2002.8 304.2 all-gather.30
  2309.0 21.9 all-gather.24
  2339.1 44.5 reduce-scatter.10
where the time goes:
time: 2400 us; the launch traced here: 2390 us
  waiting for transfers between devices  1890 us (79%)
  blocking collectives  367 us (15%)
  local copies, waits for them, and re-layouts  57 us (2%)
  matrix products  33.7 us (1%)
    all_gather x4, waiting for transfers between devices, project_in(): whole = lax.all_gather(flat, 'frame', axis=0, tiled=True)  1020 us
    all_gather x2, waiting for transfers between devices, project_out(): full_weight = lax.all_gather(weight_local, 'frame', axis=1, tiled=True)  611 us
    all_gather x2, blocking collectives, project_out(): full_weight = lax.all_gather(weight_local, 'frame', axis=1, tiled=True)  331 us
    reduce_scatter x4, waiting for transfers between devices, project_out(): lax.psum_scatter(jnp.dot(parts, full_weight, preferred_element_type=jnp.f...  173 us
    all_gather x4, waiting for transfers between devices, gather_rows(): return lax.all_gather(normed, 'row', axis=0, tiled=True)  88.2 us
  transfers between devices with their start and end apart: 15, of which 14 were waited for; matrix products, arithmetic and copies ran while one was open for 2% of the time, Pallas kernels for 0%

commit v1 on v0

v1 whole, which is shorter than its diff:
```python
import jax
import jax.numpy as jnp
from jax import lax
from jax.sharding import Mesh, PartitionSpec as P

HEADS = 16
EPSILON = 1e-06
LINE = ("xl", "xh", "c")
RING = ("xl", "xh")
PLANE = ("z", "y")
FRAME = ("z", "y", "xl")


def normalize(token_sequence, shift, scale):
    values = token_sequence.astype(jnp.float32)
    center = values - jnp.mean(values, axis=-1, keepdims=True)
    spread = jnp.mean(center * center, axis=-1, keepdims=True)
    return (center * lax.rsqrt(spread + EPSILON) * (1.0 + scale) + shift).astype(jnp.bfloat16)


def attend(query_part, key_part, value_part):
    head_size = query_part.shape[-1]
    scores = jnp.einsum(
        "blhd,bmhd->bhlm", query_part, key_part, preferred_element_type=jnp.float32
    ) * head_size ** (-0.5)
    scores = scores - jnp.max(scores, axis=-1, keepdims=True)
    raised = jnp.exp(scores)
    probs = (raised / jnp.sum(raised, axis=-1, keepdims=True)).astype(jnp.bfloat16)
    return jnp.einsum(
        "bhlm,bmhd->blhd", probs, value_part, preferred_element_type=jnp.float32
    ).astype(jnp.bfloat16)


def exchange(blocks, axes):
    return lax.all_to_all(blocks, axes, split_axis=0, concat_axis=0, tiled=True)


def spread_out(block, axes):
    count = lax.axis_size(axes)
    return exchange(jnp.broadcast_to(block[None], (count,) + block.shape), axes)


def times(tokens, weight):
    return jnp.dot(tokens, weight, preferred_element_type=jnp.float32)


def times_transposed(tokens, weight):
    return lax.dot_general(
        tokens, weight, (((1,), (1,)), ((), ())), preferred_element_type=jnp.float32
    )


def gather_line(normed):
    chips = spread_out(normed, RING)
    cores = spread_out(chips, ("c",))
    own, width = normed.shape
    cores = cores.reshape(2, 2, 2, own, width)
    return jnp.transpose(cores, (1, 2, 0, 3, 4)).reshape(-1, width)


def scatter_line(partial, own):
    width = partial.shape[-1]
    blocks = partial.astype(jnp.bfloat16).reshape(2, 2, 2, own, width)
    blocks = jnp.transpose(blocks, (2, 0, 1, 3, 4)).reshape(2, 4 * own, width)
    half = jnp.sum(exchange(blocks, ("c",)).astype(jnp.float32), axis=0).astype(jnp.bfloat16)
    quarter = exchange(half.reshape(4, own, width), RING)
    return jnp.sum(quarter.astype(jnp.float32), axis=0)


def gather_pair(normed):
    return spread_out(normed, ("c",)).reshape(-1, normed.shape[-1])


def scatter_pair(partial, own):
    width = partial.shape[-1]
    return jnp.sum(exchange(partial.reshape(2, own, width), ("c",)), axis=0)


def on_device(
    video,
    modulation,
    query_key_value_weight,
    attention_output_weight,
    feed_forward_up_weight,
    feed_forward_down_weight,
):
    stream = video[0]
    own, width = stream.shape
    head_size = width // HEADS
    depth, _, quarter = query_key_value_weight.shape[1:]
    hidden = feed_forward_up_weight.shape[2]
    output_rows = jnp.swapaxes(attention_output_weight, 1, 2)
    down_rows = jnp.swapaxes(feed_forward_down_weight, 1, 2)

    def halves(rows):
        return jnp.swapaxes(rows.reshape(depth, 2, -1), 0, 1)

    qkv = query_key_value_weight[0].reshape(depth, 3, 2, quarter // 2)
    qkv = jnp.transpose(qkv, (2, 0, 1, 3)).reshape(2, depth, -1)
    packs = jnp.concatenate(
        [qkv, halves(output_rows[0]), halves(feed_forward_up_weight[0]), halves(down_rows[0])], axis=2
    )
    packs = exchange(packs, ("xl",)).reshape(2 * depth, -1)
    first = 2 * quarter
    attention_pack = spread_out(packs[:, :first], PLANE).reshape(width, first)
    feed_pack = lax.all_gather(packs[:, first:], PLANE, axis=0, tiled=True)

    pack = jnp.concatenate(
        [
            query_key_value_weight[1].reshape(depth, -1),
            output_rows[1],
            feed_forward_up_weight[1],
            down_rows[1],
        ],
        axis=1,
    )
    pack = spread_out(pack, RING).reshape(2, 2, depth, -1)
    pack = jnp.swapaxes(pack, 1, 2).reshape(2 * depth, 2, -1)
    own_qkv = pack[:, :, : 3 * quarter].reshape(-1, 2, 3, quarter)
    rest = pack[:, :, 3 * quarter :]
    pack = jnp.concatenate(
        [
            jnp.swapaxes(own_qkv, 1, 2).reshape(2 * depth, -1),
            rest[:, :, :quarter].reshape(2 * depth, -1),
            rest[:, :, quarter : quarter + hidden].reshape(2 * depth, -1),
            rest[:, :, quarter + hidden :].reshape(2 * depth, -1),
        ],
        axis=1,
    )
    temporal_pack = lax.all_gather(pack, PLANE, axis=0, tiled=True)

    mod = modulation[0]
    local = quarter // 2
    normed = gather_line(normalize(stream, mod[0], mod[1]))
    packed = times(normed, attention_pack[:, : 3 * local]).astype(jnp.bfloat16)
    triple = packed.reshape(2, -1, 3, local // head_size, head_size)
    mixed = attend(triple[:, :, 0], triple[:, :, 1], triple[:, :, 2]).reshape(-1, local)
    update = scatter_line(times_transposed(mixed, attention_pack[:, 3 * local :]), own)
    stream = (stream.astype(jnp.float32) + mod[2] * update).astype(jnp.bfloat16)
    normed = gather_line(normalize(stream, mod[3], mod[4]))
    activated = jax.nn.gelu(times(normed, feed_pack[:, : hidden // 2]), approximate=True).astype(
        jnp.bfloat16
    )
    update = scatter_line(times_transposed(activated, feed_pack[:, hidden // 2 :]), own)
    stream = (stream.astype(jnp.float32) + mod[5] * update).astype(jnp.bfloat16)

    frames = lax.axis_size(FRAME)
    stream = exchange(stream.reshape(frames, own // frames, width), FRAME).reshape(own, width)
    mod = modulation[1]
    local = 2 * quarter
    normed = gather_pair(normalize(stream, mod[0], mod[1]))
    packed = times(normed, temporal_pack[:, : 3 * local]).astype(jnp.bfloat16)
    triple = packed.reshape(2, frames, own // frames, 3, local // head_size, head_size)
    triple = jnp.swapaxes(triple, 1, 2).reshape(-1, frames, 3, local // head_size, head_size)
    mixed = attend(triple[:, :, 0], triple[:, :, 1], triple[:, :, 2])
    mixed = jnp.swapaxes(mixed.reshape(2, own // frames, frames, local), 1, 2).reshape(-1, local)
    update = scatter_pair(times_transposed(mixed, temporal_pack[:, 3 * local : 4 * local]), own)
    stream = (stream.astype(jnp.float32) + mod[2] * update).astype(jnp.bfloat16)
    normed = gather_pair(normalize(stream, mod[3], mod[4]))
    start = 4 * local
    activated = jax.nn.gelu(
        times(normed, temporal_pack[:, start : start + 2 * hidden]), approximate=True
    ).astype(jnp.bfloat16)
    update = scatter_pair(times_transposed(activated, temporal_pack[:, start + 2 * hidden :]), own)
    stream = (stream.astype(jnp.float32) + mod[5] * update).astype(jnp.bfloat16)
    stream = exchange(stream.reshape(frames, own // frames, width), FRAME)
    return stream.reshape(1, own, width)


def solution(mesh):
    fine = Mesh(mesh.devices.reshape(8, 4, 2, 2, 2), ("z", "y", "xl", "xh", "c"))
    rows = ("xh", "c")
    in_specs = (
        P(FRAME, rows, None),
        P(),
        P(None, FRAME, None, rows),
        P(None, rows, FRAME),
        P(None, FRAME, rows),
        P(None, rows, FRAME),
    )
    out_specs = P(FRAME, rows, None)
    return jax.shard_map(
        on_device, mesh=fine, in_specs=in_specs, out_specs=out_specs, check_vma=False
    )
```

time: 2400 us -> 370 us (0.15)
  waiting for transfers between devices: 1890 us -> 85.1 us
  blocking collectives: 367 us -> 139 us
    all_gather x10 -> x2, waiting for transfers between devices: 1720 us -> 7.17 us  [the longest x1 7.17 us: on_device(): temporal_pack = lax.all_gather(pack, PLANE, axis=0, tiled=True)]
    all_gather x2 -> x0, blocking collectives: 331 us -> none  [project_out(): full_weight = lax.all_gather(weight_local, 'frame', axis=1, tiled=True)]
    reduce_scatter x4 -> x0, waiting for transfers between devices: 173 us -> none  [project_out(): lax.psum_scatter(jnp.dot(parts, full_weight, preferred_element_type=jnp.f...]
    all_to_all x1 -> x13, blocking collectives: 36.3 us -> 139 us  [exchange(): return lax.all_to_all(blocks, axes, split_axis=0, concat_axis=0, tiled=True)]
    all_to_all x1 -> x4, waiting for transfers between devices: 0.01 us -> 77.9 us  [exchange(): return lax.all_to_all(blocks, axes, split_axis=0, concat_axis=0, tiled=True)]
    all_gather x4 -> x0, local copies, waits for them, and re-layouts: 29.3 us -> none  [project_out(): full_weight = lax.all_gather(weight_local, 'frame', axis=1, tiled=True)]
  transfers between devices with their start and end apart: 15 -> 6, of which waited for: 14 -> 4; matrix products, arithmetic and copies ran while one was open for 2% -> 18% of each run, Pallas kernels for 0% -> 0%
where the time goes in v1:
time: 370 us; the launch traced here: 363 us
  blocking collectives  139 us (38%)
  waiting for transfers between devices  85.1 us (23%)
  local copies, waits for them, and re-layouts  54.5 us (15%)
  matrix products  35.1 us (9%)
  starting transfers between devices  25.5 us (7%)
  between operations  14.4 us (4%)
  other arithmetic  9.17 us (2%)
    all_to_all x13, blocking collectives, exchange(): return lax.all_to_all(blocks, axes, split_axis=0, concat_axis=0, tiled=True)  139 us
    all_to_all x4, waiting for transfers between devices, exchange(): return lax.all_to_all(blocks, axes, split_axis=0, concat_axis=0, tiled=True)  77.9 us
    all_to_all x4, starting transfers between devices, exchange(): return lax.all_to_all(blocks, axes, split_axis=0, concat_axis=0, tiled=True)  25.5 us
    unnamed x35, local copies, waits for them, and re-layouts  24.8 us
    dot_general x4, matrix products, times_transposed(): lax.dot_general(tokens, weight, (((1,), (1,)), ((), ())), preferred_eleme...  18.5 us
  transfers between devices with their start and end apart: 6, of which 4 were waited for; matrix products, arithmetic and copies ran while one was open for 18% of the time, Pallas kernels for 0%

profile of v1, /device:TPU:2, one launch (start us, length us, event | category | flops | bytes accessed | tf_op | source)
XLA Modules:
  0.0 363.3 jit_solution(5752009316367664650)
XLA Ops:
  12.1 7.3 %all_to_all.85 = bf16[2,18,1728]{2,1,0:T(8,128)(2,1)S(1)} all-to-all(bf16[2,18,1728]{2,1,0:T(8,128)(2,1)S(1)} %copy.112), channel_id=1, replica_groups=mesh['z'=8,'y'=4,'xl'=2,'xh'=2,'c'=2] {'xl'}, dimensions={0} | all-to-all | bytes 248832 | tf_op jit(solution)/shard_map/all_to_all | solution.py:35
  20.6 12.7 %all_to_all.86 = bf16[4,18,3456]{2,1,0:T(8,128)(2,1)S(1)} all-to-all(bf16[4,18,3456]{2,1,0:T(8,128)(2,1)S(1)} %broadcast_in_dim.28), channel_id=1, replica_groups=mesh['z'=8,'y'=4,'xl'=2,'xh'=2,'c'=2] {'xl','xh'}, dimensions={0} | all-to-all | bytes 995328 | tf_op jit(solution)/shard_map/all_to_all | solution.py:35
  39.0 5.0 %all-to-all-start = ((bf16[4,128,1152]{2,1,0:T(8,128)(2,1)}), bf16[4,128,1152]{2,1,0:T(8,128)(2,1)S(1)}, u32[]{:S(2)}, u32[]{:S(2)}) async-start(bf16[4,128,1152]{2,1,0:T(8,128)(2,1)} %broadcast_in_dim.21), calls=%async_computation | async-start | bytes 2359296 | tf_op jit(solution)/shard_map/all_to_all | solution.py:35
  44.0 12.3 %all-to-all-done = bf16[4,128,1152]{2,1,0:T(8,128)(2,1)S(1)} async-done(((bf16[4,128,1152]{2,1,0:T(8,128)(2,1)}), bf16[4,128,1152]{2,1,0:T(8,128)(2,1)S(1)}, u32[]{:S(2)}, u32[]{:S(2)}) %all-to-all-start) | async-done | bytes 1179680 | tf_op jit(solution)/shard_map/all_to_all | solution.py:35
  56.6 5.8 %all_to_all.87 = bf16[2,4,128,1152]{3,2,1,0:T(8,128)(2,1)S(1)} all-to-all(bf16[2,4,128,1152]{3,2,1,0:T(8,128)(2,1)S(1)} %broadcast_in_dim.22), channel_id=1, replica_groups=mesh['z'=8,'y'=4,'xl'=2,'xh'=2,'c'=2] {'c'}, dimensions={0} | all-to-all | bytes 4718592 | tf_op jit(solution)/shard_map/all_to_all | solution.py:35
  63.7 11.8 %all-to-all-start.3 = ((bf16[32,36,576]{2,1,0:T(8,128)(2,1)}), bf16[32,36,576]{2,1,0:T(8,128)(2,1)}, u32[]{:S(2)}, u32[]{:S(2)}) async-start(bf16[32,36,576]{2,1,0:T(8,128)(2,1)} %broadcast_in_dim.23), calls=%async_computation.3 | async-start | bytes 3276800 | tf_op jit(solution)/shard_map/all_to_all | solution.py:35
  77.2 51.3 %all-to-all-done.3 = bf16[32,36,576]{2,1,0:T(8,128)(2,1)} async-done(((bf16[32,36,576]{2,1,0:T(8,128)(2,1)}), bf16[32,36,576]{2,1,0:T(8,128)(2,1)}, u32[]{:S(2)}, u32[]{:S(2)}) %all-to-all-start.3) | async-done | bytes 1327136 | tf_op jit(solution)/shard_map/all_to_all | solution.py:35
  143.3 5.6 %all_to_all.88 = bf16[2,512,1152]{2,1,0:T(8,128)(2,1)S(1)} all-to-all(bf16[2,512,1152]{2,1,0:T(8,128)(2,1)S(1)} %bitcast.150), channel_id=1, replica_groups=mesh['z'=8,'y'=4,'xl'=2,'xh'=2,'c'=2] {'c'}, dimensions={0} | all-to-all | bytes 4718592 | tf_op jit(solution)/shard_map/all_to_all | solution.py:35
  150.7 19.8 %all_to_all.89 = bf16[4,128,1152]{2,1,0:T(8,128)(2,1)S(1)} all-to-all(bf16[4,128,1152]{2,1,0:T(8,128)(2,1)} %bitcast.154), channel_id=1, replica_groups=mesh['z'=8,'y'=4,'xl'=2,'xh'=2,'c'=2] {'xl','xh'}, dimensions={0} | all-to-all | bytes 2359296 | tf_op jit(solution)/shard_map/all_to_all | solution.py:35
  171.4 18.4 %all_to_all.90 = bf16[4,128,1152]{2,1,0:T(8,128)(2,1)S(1)} all-to-all(bf16[4,128,1152]{2,1,0:T(8,128)(2,1)S(1)} %broadcast_in_dim.25), channel_id=1, replica_groups=mesh['z'=8,'y'=4,'xl'=2,'xh'=2,'c'=2] {'xl','xh'}, dimensions={0} | all-to-all | bytes 2359296 | tf_op jit(solution)/shard_map/all_to_all | solution.py:35
  190.1 5.8 %all_to_all.91 = bf16[2,4,128,1152]{3,2,1,0:T(8,128)(2,1)S(1)} all-to-all(bf16[2,4,128,1152]{3,2,1,0:T(8,128)(2,1)S(1)} %broadcast_in_dim.26), channel_id=1, replica_groups=mesh['z'=8,'y'=4,'xl'=2,'xh'=2,'c'=2] {'c'}, dimensions={0} | all-to-all | bytes 4718592 | tf_op jit(solution)/shard_map/all_to_all | solution.py:35
  201.2 7.5 %convolution_convert_fusion = bf16[1024,1152]{1,0:T(8,128)(2,1)} fusion(bf16[1152,1152]{1,0:T(8,128)(2,1)S(1)} %reshape.550, bf16[1024,1152]{1,0:T(8,128)(2,1)} %bitcast.160), kind=kOutput, calls=%fused_computation.10 | convolution fusion | flops 2724397056 | bytes 7667712 | tf_op jit(solution)/shard_map/dot_general | solution.py:48
  210.6 5.6 %all_to_all.92 = bf16[2,512,1152]{2,1,0:T(8,128)(2,1)S(1)} all-to-all(bf16[2,512,1152]{2,1,0:T(8,128)(2,1)S(1)} %bitcast.151), channel_id=1, replica_groups=mesh['z'=8,'y'=4,'xl'=2,'xh'=2,'c'=2] {'c'}, dimensions={0} | all-to-all | bytes 4718592 | tf_op jit(solution)/shard_map/all_to_all | solution.py:35
  218.1 5.0 %all-to-all-start.9 = ((bf16[4,128,1152]{2,1,0:T(8,128)(2,1)}), bf16[4,128,1152]{2,1,0:T(8,128)(2,1)S(1)}, u32[]{:S(2)}, u32[]{:S(2)}) async-start(bf16[4,128,1152]{2,1,0:T(8,128)(2,1)} %bitcast.153), calls=%async_computation.9 | async-start | bytes 2359296 | tf_op jit(solution)/shard_map/all_to_all | solution.py:35
  223.7 14.4 %all-to-all-done.9 = bf16[4,128,1152]{2,1,0:T(8,128)(2,1)S(1)} async-done(((bf16[4,128,1152]{2,1,0:T(8,128)(2,1)}), bf16[4,128,1152]{2,1,0:T(8,128)(2,1)S(1)}, u32[]{:S(2)}, u32[]{:S(2)}) %all-to-all-start.9) | async-done | bytes 1179680 | tf_op jit(solution)/shard_map/all_to_all | solution.py:35
  239.0 24.2 %all_to_all.93 = bf16[64,2,1152]{2,1,0:T(2,128)(2,1)S(1)} all-to-all(bf16[64,2,1152]{2,1,0:T(2,128)(2,1)S(1)} %add_convert_fusion.4), channel_id=1, replica_groups=mesh['z'=8,'y'=4,'xl'=2,'xh'=2,'c'=2] {'z','y','xl'}, dimensions={0} | all-to-all | bytes 589824 | tf_op jit(solution)/shard_map/all_to_all | solution.py:35
  269.3 7.2 %all-gather.7.cloned.1.call-done = bf16[32,36,6912]{2,1,0:T(8,128)(2,1)} async-done(((bf16[1,36,6912]{2,1,0:T(8,128)(2,1)}), bf16[32,36,6912]{2,1,0:T(8,128)(2,1)}) %all-gather.7.cloned.1.call-update) | async-done | bytes 15925264 | tf_op jit(solution)/shard_map/all_gather | solution.py:130
  276.4 18.4 %reshape.552 = bf16[1152,6912]{1,0:T(8,128)(2,1)} reshape(bf16[32,36,6912]{2,1,0:T(8,128)(2,1)} %all-gather.7.cloned.1.call-done) | data formatting | bytes 31850496
  294.9 3.9 %fusion.11 = bf16[256,1728]{0,1:T(8,128)(2,1)S(1)} fusion(bf16[256,1152]{1,0:T(8,128)(2,1)S(1)} %bitcast.176, bf16[1152,6912]{1,0:T(8,128)(2,1)} %reshape.552), kind=kOutput, calls=%fused_computation.16 | convolution fusion | flops 1019658240 | bytes 5603328 | tf_op jit(solution)/shard_map/dot_general | solution.py:44
  310.7 4.7 %all_to_all.94 = f32[2,128,1152]{2,1,0:T(8,128)S(1)} all-to-all(f32[2,128,1152]{2,1,0:T(8,128)S(1)} %fusion.39), channel_id=1, replica_groups=mesh['z'=8,'y'=4,'xl'=2,'xh'=2,'c'=2] {'c'}, dimensions={0} | all-to-all | bytes 2359296 | tf_op jit(solution)/shard_map/all_to_all | solution.py:35
  317.4 4.2 %all_to_all.95 = bf16[2,128,1152]{2,1,0:T(8,128)(2,1)S(1)} all-to-all(bf16[2,128,1152]{2,1,0:T(8,128)(2,1)S(1)} %broadcast_in_dim.29), channel_id=1, replica_groups=mesh['z'=8,'y'=4,'xl'=2,'xh'=2,'c'=2] {'c'}, dimensions={0} | all-to-all | bytes 1179648 | tf_op jit(solution)/shard_map/all_to_all | solution.py:35
  321.7 7.5 %fusion.2 = f32[256,1152]{1,0:T(8,128)S(1)} fusion(bf16[1152,6912]{1,0:T(8,128)(2,1)} %reshape.552, bf16[256,1152]{1,0:T(8,128)(2,1)S(1)} %bitcast.177), kind=kOutput, calls=%fused_computation.2 | convolution fusion | flops 2723217408 | bytes 12386304 | tf_op jit(solution)/shard_map/dot_general | solution.py:48
  329.1 4.7 %all_to_all.96 = f32[2,128,1152]{2,1,0:T(8,128)S(1)} all-to-all(f32[2,128,1152]{2,1,0:T(8,128)S(1)} %bitcast.169), channel_id=1, replica_groups=mesh['z'=8,'y'=4,'xl'=2,'xh'=2,'c'=2] {'c'}, dimensions={0} | all-to-all | bytes 2359296 | tf_op jit(solution)/shard_map/all_to_all | solution.py:35
  334.6 20.5 %all_to_all.97 = bf16[64,2,1152]{2,1,0:T(2,128)(2,1)S(1)} all-to-all(bf16[64,2,1152]{2,1,0:T(2,128)(2,1)S(1)} %fusion.60), channel_id=1, replica_groups=mesh['z'=8,'y'=4,'xl'=2,'xh'=2,'c'=2] {'z','y','xl'}, dimensions={0} | all-to-all | bytes 589824 | tf_op jit(solution)/shard_map/all_to_all | solution.py:35
  (137 shorter events, 65.3 us)
Async XLA Ops:
  6.5 191.0 %all-gather.5.cloned.1.call-start = ((), (), s32[]{:S(2)}) async-start(), calls=%async_computation.17 | async-start | bytes 3041280 | tf_op jit(solution)/shard_map/all_gather | solution.py:106
  19.5 24.5 %copy-start.2 = (bf16[36,1728]{1,0:T(8,128)(2,1)}, bf16[36,1728]{1,0:T(8,128)(2,1)S(1)}, u32[]{:S(2)}) copy-start(bf16[36,1728]{1,0:T(8,128)(2,1)S(1)} %reshape.521) | copy-start | bytes 373252
  20.3 256.2 %all-gather.7.cloned.1.call-start = ((), (), s32[]{:S(2)}) async-start(), calls=%async_computation.18 | async-start | bytes 18247680 | tf_op jit(solution)/shard_map/all_gather | solution.py:130
  34.2 2.2 copy-start.3
  34.2 3.0 copy-start
  39.0 17.3 %all-to-all-start = ((bf16[4,128,1152]{2,1,0:T(8,128)(2,1)}), bf16[4,128,1152]{2,1,0:T(8,128)(2,1)S(1)}, u32[]{:S(2)}, u32[]{:S(2)}) async-start(bf16[4,128,1152]{2,1,0:T(8,128)(2,1)} %broadcast_in_dim.21), calls=%async_computation | async-start | bytes 2359296 | tf_op jit(solution)/shard_map/all_to_all | solution.py:35
  56.6 5.8 %slice-start = ((bf16[36,1728]{1,0:T(8,128)(2,1)}), bf16[36,576]{1,0:T(8,128)(2,1)S(1)}, s32[]{:S(2)}) async-start(bf16[36,1728]{1,0:T(8,128)(2,1)} %copy-done.2), calls=%async_computation.19 | async-start | bytes 102400 | tf_op jit(solution)/shard_map/slice | solution.py:105
  63.7 64.7 %all-to-all-start.3 = ((bf16[32,36,576]{2,1,0:T(8,128)(2,1)}), bf16[32,36,576]{2,1,0:T(8,128)(2,1)}, u32[]{:S(2)}, u32[]{:S(2)}) async-start(bf16[32,36,576]{2,1,0:T(8,128)(2,1)} %broadcast_in_dim.23), calls=%async_computation.3 | async-start | bytes 3276800 | tf_op jit(solution)/shard_map/all_to_all | solution.py:35
  150.7 20.4 %copy-start.10 = (f32[1152]{0:T(1024)S(1)}, f32[1152]{0:T(1024)}, u32[]{:S(2)}) copy-start(f32[1152]{0:T(1024)} %get-tuple-element.11) | copy-start | bytes 13828
  150.7 20.4 %copy-start.11 = (f32[1152]{0:T(1024)S(1)}, f32[1152]{0:T(1024)}, u32[]{:S(2)}) copy-start(f32[1152]{0:T(1024)} %get-tuple-element.12) | copy-start | bytes 13828
  218.1 20.0 %all-to-all-start.9 = ((bf16[4,128,1152]{2,1,0:T(8,128)(2,1)}), bf16[4,128,1152]{2,1,0:T(8,128)(2,1)S(1)}, u32[]{:S(2)}, u32[]{:S(2)}) async-start(bf16[4,128,1152]{2,1,0:T(8,128)(2,1)} %bitcast.153), calls=%async_computation.9 | async-start | bytes 2359296 | tf_op jit(solution)/shard_map/all_to_all | solution.py:35
  223.1 15.5 %copy-start.9 = (f32[1152]{0:T(1024)S(1)}, f32[1152]{0:T(1024)}, u32[]{:S(2)}) copy-start(f32[1152]{0:T(1024)} %get-tuple-element.13) | copy-start | bytes 13828
  238.6 25.9 %copy-start.7 = (f32[1152]{0:T(1024)S(1)}, f32[1152]{0:T(1024)}, u32[]{:S(2)}) copy-start(f32[1152]{0:T(1024)} %get-tuple-element.8) | copy-start | bytes 13828
  238.6 25.9 %copy-start.8 = (f32[1152]{0:T(1024)S(1)}, f32[1152]{0:T(1024)}, u32[]{:S(2)}) copy-start(f32[1152]{0:T(1024)} %get-tuple-element.9) | copy-start | bytes 13828
  265.5 29.4 %all-to-all-start.11 = ((bf16[2,128,1152]{2,1,0:T(8,128)(2,1)}), bf16[2,128,1152]{2,1,0:T(8,128)(2,1)S(1)}, u32[]{:S(2)}, u32[]{:S(2)}) async-start(bf16[2,128,1152]{2,1,0:T(8,128)(2,1)} %broadcast_in_dim.27), calls=%async_computation.11 | async-start | bytes 1179648 | tf_op jit(solution)/shard_map/all_to_all | solution.py:35
  302.8 1.8 copy-start.1
  315.3 1.8 copy-start.5
  315.4 1.9 copy-start.6
  329.1 5.2 %copy-start.4 = (f32[1152]{0:T(1024)S(1)}, f32[1152]{0:T(1024)}, u32[]{:S(2)}) copy-start(f32[1152]{0:T(1024)} %get-tuple-element.7) | copy-start | bytes 13828
Sparse Core Ops, SparseCore 0:
  20.4 102.5 all-gather.4
  125.6 150.8 all-gather.6

commit v2 on v1

--- a/solution.py
+++ b/solution.py
@@ -1,5 +1,6 @@
 import jax
 import jax.numpy as jnp
+import numpy as np
 from jax import lax
 from jax.sharding import Mesh, PartitionSpec as P
 
@@ -7,8 +8,8 @@
 EPSILON = 1e-06
 LINE = ("xl", "xh", "c")
 RING = ("xl", "xh")
-PLANE = ("z", "y")
-FRAME = ("z", "y", "xl")
+PLANE = ("zh", "zl", "y")
+FRAME = ("zh", "zl", "y", "xl")
 
 
 def normalize(token_sequence, shift, scale):
@@ -89,45 +90,63 @@
     head_size = width // HEADS
     depth, _, quarter = query_key_value_weight.shape[1:]
     hidden = feed_forward_up_weight.shape[2]
+    order = np.arange(width).reshape(2, 16, -1).swapaxes(0, 1).reshape(-1)
+    inner = jnp.asarray(np.eye(width)[:, order], jnp.bfloat16)
+    stream = times(stream, inner).astype(jnp.bfloat16)
+    modulation = jnp.swapaxes(modulation.reshape(2, 6, 2, 16, -1), 2, 3).reshape(2, 6, width)
     output_rows = jnp.swapaxes(attention_output_weight, 1, 2)
     down_rows = jnp.swapaxes(feed_forward_down_weight, 1, 2)
 
     def halves(rows):
         return jnp.swapaxes(rows.reshape(depth, 2, -1), 0, 1)
 
-    qkv = query_key_value_weight[0].reshape(depth, 3, 2, quarter // 2)
-    qkv = jnp.transpose(qkv, (2, 0, 1, 3)).reshape(2, depth, -1)
-    packs = jnp.concatenate(
-        [qkv, halves(output_rows[0]), halves(feed_forward_up_weight[0]), halves(down_rows[0])], axis=2
-    )
-    packs = exchange(packs, ("xl",)).reshape(2 * depth, -1)
-    first = 2 * quarter
-    attention_pack = spread_out(packs[:, :first], PLANE).reshape(width, first)
-    feed_pack = lax.all_gather(packs[:, first:], PLANE, axis=0, tiled=True)
+    def split_qkv(weight):
+        parts = weight.reshape(depth, 3, 2, quarter // 2)
+        return jnp.transpose(parts, (2, 0, 1, 3)).reshape(2, depth, -1)
+
+    def spread_plane(packs):
+        columns = packs.shape[-1]
+        lines = lax.axis_size(("zh", "zl"))
+        packs = jnp.broadcast_to(packs[None], (lines,) + packs.shape)
+        packs = exchange(packs.reshape(2 * lines, depth, columns), ("zh", "zl", "xl"))
+        packs = spread_out(packs.reshape(-1, columns), ("y",))
+        packs = packs.reshape(4, 2, 4, 2 * depth, columns)
+        return jnp.transpose(packs, (2, 0, 1, 3, 4)).reshape(width, columns)
+
+    attention_pack = spread_plane(
+        jnp.concatenate([split_qkv(query_key_value_weight[0]), halves(output_rows[0])], axis=2)
+    )
 
     pack = jnp.concatenate(
         [
-            query_key_value_weight[1].reshape(depth, -1),
-            output_rows[1],
-            feed_forward_up_weight[1],
-            down_rows[1],
+            halves(feed_forward_up_weight[1]),
+            halves(down_rows[1]),
+            split_qkv(query_key_value_weight[1]),
+            halves(output_rows[1]),
+        ],
+        axis=2,
+    )
+    pack = jnp.broadcast_to(pack[:, None], (2, 4) + pack.shape[1:]).reshape(8, depth, -1)
+    pack = exchange(pack, ("zh", "xl", "xh")).reshape(4, 2, depth, -1)
+    pack = jnp.transpose(pack, (0, 2, 1, 3)).reshape(4 * depth, 2, -1)
+    half_hidden = hidden // 2
+    half = quarter // 2
+    qkv_start = 2 * half_hidden
+    qkv = pack[:, :, qkv_start : qkv_start + 3 * half].reshape(-1, 2, 3, half)
+    pack = jnp.concatenate(
+        [
+            pack[:, :, :half_hidden].reshape(4 * depth, -1),
+            pack[:, :, half_hidden:qkv_start].reshape(4 * depth, -1),
+            jnp.swapaxes(qkv, 1, 2).reshape(4 * depth, -1),
+            pack[:, :, qkv_start + 3 * half :].reshape(4 * depth, -1),
         ],
         axis=1,
     )
-    pack = spread_out(pack, RING).reshape(2, 2, depth, -1)
-    pack = jnp.swapaxes(pack, 1, 2).reshape(2 * depth, 2, -1)
-    own_qkv = pack[:, :, : 3 * quarter].reshape(-1, 2, 3, quarter)
-    rest = pack[:, :, 3 * quarter :]
-    pack = jnp.concatenate(
-        [
-            jnp.swapaxes(own_qkv, 1, 2).reshape(2 * depth, -1),
-            rest[:, :, :quarter].reshape(2 * depth, -1),
-            rest[:, :, quarter : quarter + hidden].reshape(2 * depth, -1),
-            rest[:, :, quarter + hidden :].reshape(2 * depth, -1),
-        ],
-        axis=1,
-    )
-    temporal_pack = lax.all_gather(pack, PLANE, axis=0, tiled=True)
+    temporal_packs = lax.all_gather(pack, PLANE, axis=0).reshape(2, width, -1)
+
+    feed_pack = spread_plane(
+        jnp.concatenate([halves(feed_forward_up_weight[0]), halves(down_rows[0])], axis=2)
+    )
 
     mod = modulation[0]
     local = quarter // 2
@@ -147,28 +166,33 @@
     frames = lax.axis_size(FRAME)
     stream = exchange(stream.reshape(frames, own // frames, width), FRAME).reshape(own, width)
     mod = modulation[1]
-    local = 2 * quarter
+    local = quarter
+    heads = local // head_size
     normed = gather_pair(normalize(stream, mod[0], mod[1]))
-    packed = times(normed, temporal_pack[:, : 3 * local]).astype(jnp.bfloat16)
-    triple = packed.reshape(2, frames, own // frames, 3, local // head_size, head_size)
-    triple = jnp.swapaxes(triple, 1, 2).reshape(-1, frames, 3, local // head_size, head_size)
-    mixed = attend(triple[:, :, 0], triple[:, :, 1], triple[:, :, 2])
-    mixed = jnp.swapaxes(mixed.reshape(2, own // frames, frames, local), 1, 2).reshape(-1, local)
-    update = scatter_pair(times_transposed(mixed, temporal_pack[:, 3 * local : 4 * local]), own)
-    stream = (stream.astype(jnp.float32) + mod[2] * update).astype(jnp.bfloat16)
+    update = 0.0
+    for group in range(2):
+        weights = temporal_packs[group][:, 2 * hidden :]
+        packed = times(normed, weights[:, : 3 * local]).astype(jnp.bfloat16)
+        triple = packed.reshape(2, frames, own // frames, 3, heads, head_size)
+        triple = jnp.swapaxes(triple, 1, 2).reshape(-1, frames, 3, heads, head_size)
+        mixed = attend(triple[:, :, 0], triple[:, :, 1], triple[:, :, 2])
+        mixed = jnp.swapaxes(mixed.reshape(2, own // frames, frames, local), 1, 2)
+        update += times_transposed(mixed.reshape(-1, local), weights[:, 3 * local :])
+    stream = (stream.astype(jnp.float32) + mod[2] * scatter_pair(update, own)).astype(jnp.bfloat16)
     normed = gather_pair(normalize(stream, mod[3], mod[4]))
-    start = 4 * local
-    activated = jax.nn.gelu(
-        times(normed, temporal_pack[:, start : start + 2 * hidden]), approximate=True
-    ).astype(jnp.bfloat16)
-    update = scatter_pair(times_transposed(activated, temporal_pack[:, start + 2 * hidden :]), own)
-    stream = (stream.astype(jnp.float32) + mod[5] * update).astype(jnp.bfloat16)
+    update = 0.0
+    for group in range(2):
+        weights = temporal_packs[group][:, : 2 * hidden]
+        activated = jax.nn.gelu(times(normed, weights[:, :hidden]), approximate=True)
+        update += times_transposed(activated.astype(jnp.bfloat16), weights[:, hidden:])
+    stream = (stream.astype(jnp.float32) + mod[5] * scatter_pair(update, own)).astype(jnp.bfloat16)
+    stream = times_transposed(stream, inner).astype(jnp.bfloat16)
     stream = exchange(stream.reshape(frames, own // frames, width), FRAME)
     return stream.reshape(1, own, width)
 
 
 def solution(mesh):
-    fine = Mesh(mesh.devices.reshape(8, 4, 2, 2, 2), ("z", "y", "xl", "xh", "c"))
+    fine = Mesh(mesh.devices.reshape(2, 4, 4, 2, 2, 2), ("zh", "zl", "y", "xl", "xh", "c"))
     rows = ("xh", "c")
     in_specs = (
         P(FRAME, rows, None),

time: 370 us -> 447 us (1.21)
  waiting for transfers between devices: 85.1 us -> 164 us
  blocking collectives: 139 us -> 88.3 us
  starting transfers between devices: 25.5 us -> 54.4 us
  matrix products: 35.1 us -> 47.2 us
    all_to_all x4 -> x9, waiting for transfers between devices: 77.9 us -> 164 us  [exchange(): return lax.all_to_all(blocks, axes, split_axis=0, concat_axis=0, tiled=True)]
    all_to_all x13 -> x10, blocking collectives: 139 us -> 88.3 us  [exchange(): return lax.all_to_all(blocks, axes, split_axis=0, concat_axis=0, tiled=True)]
    all_to_all x4 -> x9, starting transfers between devices: 25.5 us -> 54.4 us  [exchange(): return lax.all_to_all(blocks, axes, split_axis=0, concat_axis=0, tiled=True)]
    unnamed x35 -> x51, local copies, waits for them, and re-layouts: 24.8 us -> 1.17 us
    dot_general x4 -> x7, matrix products: 18.5 us -> 25.7 us  [times_transposed(): lax.dot_general(tokens, weight, (((1,), (1,)), ((), ())), preferred_eleme...]
    all_gather x2 -> x1, waiting for transfers between devices: 7.17 us -> 0.01 us  [on_device(): temporal_packs = lax.all_gather(pack, PLANE, axis=0).reshape(2, width, -1)]
    broadcast_in_dim x8 -> x10, local copies, waits for them, and re-layouts: 4.19 us -> 10.5 us  [spread_out(): return exchange(jnp.broadcast_to(block[None], (count,) + block.shape), axes)]
    reshape x8 -> x18, local copies, waits for them, and re-layouts: 5.39 us -> 11.1 us  [the longest x2 3.75 us: spread_plane(): return jnp.transpose(packs, (2, 0, 1, 3, 4)).reshape(width, columns)]
  transfers between devices with their start and end apart: 6 -> 10, of which waited for: 4 -> 9; matrix products, arithmetic and copies ran while one was open for 18% -> 15% of each run, Pallas kernels for 0% -> 0%
where the time goes in v2:
time: 447 us; the launch traced here: 439 us
  waiting for transfers between devices  164 us (37%)
  blocking collectives  88.3 us (20%)
  local copies, waits for them, and re-layouts  58.2 us (13%)
  starting transfers between devices  54.4 us (12%)
  matrix products  47.2 us (11%)
  between operations  14.4 us (3%)
  other arithmetic  12.4 us (3%)
    all_to_all x9, waiting for transfers between devices, exchange(): return lax.all_to_all(blocks, axes, split_axis=0, concat_axis=0, tiled=True)  164 us
    all_to_all x10, blocking collectives, exchange(): return lax.all_to_all(blocks, axes, split_axis=0, concat_axis=0, tiled=True)  88.3 us
    all_to_all x9, starting transfers between devices, exchange(): return lax.all_to_all(blocks, axes, split_axis=0, concat_axis=0, tiled=True)  54.4 us
    dot_general x7, matrix products, times_transposed(): lax.dot_general(tokens, weight, (((1,), (1,)), ((), ())), preferred_eleme...  25.7 us
    broadcast_in_dim x10, local copies, waits for them, and re-layouts, spread_out(): return exchange(jnp.broadcast_to(block[None], (count,) + block.shape), axes)  10.5 us
    dot_general x4, matrix products, times(): return jnp.dot(tokens, weight, preferred_element_type=jnp.float32)  9.3 us
  transfers between devices with their start and end apart: 10, of which 9 were waited for; matrix products, arithmetic and copies ran while one was open for 15% of the time, Pallas kernels for 0%

profile of v2, /device:TPU:2, one launch (start us, length us, event | category | flops | bytes accessed | tf_op | source)
XLA Modules:
  0.0 438.7 jit_solution(2543440350133772724)
XLA Ops:
  15.3 26.5 %all_to_all.95 = bf16[8,18,1728]{2,1,0:T(8,128)(2,1)S(1)} all-to-all(bf16[8,18,1728]{2,1,0:T(8,128)(2,1)S(1)} %bitcast.179), channel_id=1, replica_groups=mesh['zh'=2,'zl'=4,'y'=4,'xl'=2,'xh'=2,'c'=2] {'zh','xl','xh'}, dimensions={0} | all-to-all | bytes 995328 | tf_op jit(solution)/shard_map/all_to_all | solution.py:36
  50.1 10.5 %all-to-all-start.2 = ((bf16[16,18,576]{2,1,0:T(8,128)(2,1)}), bf16[16,18,576]{2,1,0:T(8,128)(2,1)}, u32[]{:S(2)}, u32[]{:S(2)}) async-start(bf16[16,18,576]{2,1,0:T(8,128)(2,1)} %bitcast.10), calls=%async_computation.2 | async-start | bytes 983040 | tf_op jit(solution)/shard_map/all_to_all | solution.py:36
  65.0 14.8 %all-to-all-done.2 = bf16[16,18,576]{2,1,0:T(8,128)(2,1)} async-done(((bf16[16,18,576]{2,1,0:T(8,128)(2,1)}), bf16[16,18,576]{2,1,0:T(8,128)(2,1)}, u32[]{:S(2)}, u32[]{:S(2)}) %all-to-all-start.2) | async-done | bytes 331808 | tf_op jit(solution)/shard_map/all_to_all | solution.py:36
  87.5 7.6 %all-to-all-done = bf16[4,128,1152]{2,1,0:T(8,128)(2,1)S(1)} async-done(((bf16[4,128,1152]{2,1,0:T(8,128)(2,1)}), bf16[4,128,1152]{2,1,0:T(8,128)(2,1)S(1)}, u32[]{:S(2)}, u32[]{:S(2)}) %all-to-all-start) | async-done | bytes 1179680 | tf_op jit(solution)/shard_map/all_to_all | solution.py:36
  95.4 5.8 %all_to_all.96 = bf16[2,4,128,1152]{3,2,1,0:T(8,128)(2,1)S(1)} all-to-all(bf16[2,4,128,1152]{3,2,1,0:T(8,128)(2,1)S(1)} %broadcast_in_dim.27), channel_id=1, replica_groups=mesh['zh'=2,'zl'=4,'y'=4,'xl'=2,'xh'=2,'c'=2] {'c'}, dimensions={0} | all-to-all | bytes 4718592 | tf_op jit(solution)/shard_map/all_to_all | solution.py:36
  109.3 34.2 %all-to-all-done.3 = bf16[4,288,576]{2,1,0:T(8,128)(2,1)} async-done(((bf16[4,288,576]{2,1,0:T(8,128)(2,1)}), bf16[4,288,576]{2,1,0:T(8,128)(2,1)}, u32[]{:S(2)}, u32[]{:S(2)}) %all-to-all-start.3) | async-done | bytes 1327136 | tf_op jit(solution)/shard_map/all_to_all | solution.py:36
  161.1 5.6 %all_to_all.97 = bf16[2,512,1152]{2,1,0:T(8,128)(2,1)S(1)} all-to-all(bf16[2,512,1152]{2,1,0:T(8,128)(2,1)S(1)} %bitcast.170), channel_id=1, replica_groups=mesh['zh'=2,'zl'=4,'y'=4,'xl'=2,'xh'=2,'c'=2] {'c'}, dimensions={0} | all-to-all | bytes 4718592 | tf_op jit(solution)/shard_map/all_to_all | solution.py:36
  167.8 6.3 %all-to-all-start.8 = ((bf16[16,18,1152]{2,1,0:T(8,128)(2,1)}), bf16[16,18,1152]{2,1,0:T(8,128)(2,1)}, u32[]{:S(2)}, u32[]{:S(2)}) async-start(bf16[16,18,1152]{2,1,0:T(8,128)(2,1)} %bitcast.176), calls=%async_computation.8 | async-start | bytes 1769472 | tf_op jit(solution)/shard_map/all_to_all | solution.py:36
  175.8 31.3 %all-to-all-done.8 = bf16[16,18,1152]{2,1,0:T(8,128)(2,1)} async-done(((bf16[16,18,1152]{2,1,0:T(8,128)(2,1)}), bf16[16,18,1152]{2,1,0:T(8,128)(2,1)}, u32[]{:S(2)}, u32[]{:S(2)}) %all-to-all-start.8) | async-done | bytes 663584 | tf_op jit(solution)/shard_map/all_to_all | solution.py:36
  207.1 5.0 %all-to-all-start.5 = ((bf16[4,128,1152]{2,1,0:T(8,128)(2,1)}), bf16[4,128,1152]{2,1,0:T(8,128)(2,1)S(1)}, u32[]{:S(2)}, u32[]{:S(2)}) async-start(bf16[4,128,1152]{2,1,0:T(8,128)(2,1)} %bitcast.174), calls=%async_computation.5 | async-start | bytes 2359296 | tf_op jit(solution)/shard_map/all_to_all | solution.py:36
  213.4 12.5 %all-to-all-done.5 = bf16[4,128,1152]{2,1,0:T(8,128)(2,1)S(1)} async-done(((bf16[4,128,1152]{2,1,0:T(8,128)(2,1)}), bf16[4,128,1152]{2,1,0:T(8,128)(2,1)S(1)}, u32[]{:S(2)}, u32[]{:S(2)}) %all-to-all-start.5) | async-done | bytes 1179680 | tf_op jit(solution)/shard_map/all_to_all | solution.py:36
  236.6 27.0 %all-to-all-done.9 = bf16[4,288,1152]{2,1,0:T(8,128)(2,1)S(1)} async-done(((bf16[4,288,1152]{2,1,0:T(8,128)(2,1)}), bf16[4,288,1152]{2,1,0:T(8,128)(2,1)S(1)}, u32[]{:S(2)}, u32[]{:S(2)}) %all-to-all-start.9) | async-done | bytes 2654240 | tf_op jit(solution)/shard_map/all_to_all | solution.py:36
  264.7 6.6 %all-to-all-start.6 = ((bf16[4,128,1152]{2,1,0:T(8,128)(2,1)}), bf16[4,128,1152]{2,1,0:T(8,128)(2,1)}, u32[]{:S(2)}, u32[]{:S(2)}) async-start(bf16[4,128,1152]{2,1,0:T(8,128)(2,1)} %broadcast_in_dim.31), calls=%async_computation.6 | async-start | bytes 2359296 | tf_op jit(solution)/shard_map/all_to_all | solution.py:36
  275.3 9.7 %all-to-all-done.6 = bf16[4,128,1152]{2,1,0:T(8,128)(2,1)} async-done(((bf16[4,128,1152]{2,1,0:T(8,128)(2,1)}), bf16[4,128,1152]{2,1,0:T(8,128)(2,1)}, u32[]{:S(2)}, u32[]{:S(2)}) %all-to-all-start.6) | async-done | bytes 1179680 | tf_op jit(solution)/shard_map/all_to_all | solution.py:36
  286.6 5.6 %all_to_all.98 = bf16[2,4,128,1152]{3,2,1,0:T(8,128)(2,1)S(1)} all-to-all(bf16[2,4,128,1152]{3,2,1,0:T(8,128)(2,1)S(1)} %broadcast_in_dim.32), channel_id=1, replica_groups=mesh['zh'=2,'zl'=4,'y'=4,'xl'=2,'xh'=2,'c'=2] {'c'}, dimensions={0} | all-to-all | bytes 4718592 | tf_op jit(solution)/shard_map/all_to_all | solution.py:36
  294.8 7.4 %convolution_convert_fusion = bf16[1024,1152]{1,0:T(8,128)(2,1)} fusion(bf16[1152,1152]{1,0:T(8,128)(2,1)S(1)} %copy-done.5, bf16[1024,1152]{1,0:T(8,128)(2,1)} %bitcast.185), kind=kOutput, calls=%fused_computation.5 | convolution fusion | flops 2724397056 | bytes 7667712 | tf_op jit(solution)/shard_map/dot_general | solution.py:49
  304.1 5.6 %all_to_all.99 = bf16[2,512,1152]{2,1,0:T(8,128)(2,1)S(1)} all-to-all(bf16[2,512,1152]{2,1,0:T(8,128)(2,1)S(1)} %bitcast.171), channel_id=1, replica_groups=mesh['zh'=2,'zl'=4,'y'=4,'xl'=2,'xh'=2,'c'=2] {'c'}, dimensions={0} | all-to-all | bytes 4718592 | tf_op jit(solution)/shard_map/all_to_all | solution.py:36
  311.5 5.3 %all-to-all-start.11 = ((bf16[4,128,1152]{2,1,0:T(8,128)(2,1)}), bf16[4,128,1152]{2,1,0:T(8,128)(2,1)S(1)}, u32[]{:S(2)}, u32[]{:S(2)}) async-start(bf16[4,128,1152]{2,1,0:T(8,128)(2,1)} %bitcast.175), calls=%async_computation.11 | async-start | bytes 2359296 | tf_op jit(solution)/shard_map/all_to_all | solution.py:36
  316.9 14.9 %all-to-all-done.11 = bf16[4,128,1152]{2,1,0:T(8,128)(2,1)S(1)} async-done(((bf16[4,128,1152]{2,1,0:T(8,128)(2,1)}), bf16[4,128,1152]{2,1,0:T(8,128)(2,1)S(1)}, u32[]{:S(2)}, u32[]{:S(2)}) %all-to-all-start.11) | async-done | bytes 1179680 | tf_op jit(solution)/shard_map/all_to_all | solution.py:36
  332.9 7.6 %all-to-all-start.12 = ((bf16[64,2,1152]{2,1,0:T(2,128)(2,1)}), bf16[64,2,1152]{2,1,0:T(2,128)(2,1)S(1)}, u32[]{:S(2)}, u32[]{:S(2)}) async-start(bf16[64,2,1152]{2,1,0:T(2,128)(2,1)} %reshape.483), calls=%async_computation.12 | async-start | bytes 589824 | tf_op jit(solution)/shard_map/all_to_all | solution.py:36
  341.7 11.9 %all-to-all-done.12 = bf16[64,2,1152]{2,1,0:T(2,128)(2,1)S(1)} async-done(((bf16[64,2,1152]{2,1,0:T(2,128)(2,1)}), bf16[64,2,1152]{2,1,0:T(2,128)(2,1)S(1)}, u32[]{:S(2)}, u32[]{:S(2)}) %all-to-all-start.12) | async-done | bytes 294944 | tf_op jit(solution)/shard_map/all_to_all | solution.py:36
  394.6 5.5 %convolution_add_fusion = f32[256,1152]{1,0:T(8,128)} fusion(f32[256,1152]{1,0:T(8,128)S(1)} %fusion.9, bf16[2304,3456]{1,0:T(8,128)(2,1)} %all-gather.3.cloned.1.call-done, bf16[256,1152]{1,0:T(8,128)(2,1)S(1)} %bitcast.203), kind=kOutput, calls=%fused_computation.10 | convolution fusion | flops 1361903616 | bytes 8257536 | tf_op jit(solution)/shard_map/dot_general | solution.py:49
  400.1 6.9 %all_to_all.103 = f32[2,128,1152]{2,1,0:T(8,128)} all-to-all(f32[2,128,1152]{2,1,0:T(8,128)} %bitcast.194), channel_id=1, replica_groups=mesh['zh'=2,'zl'=4,'y'=4,'xl'=2,'xh'=2,'c'=2] {'c'}, dimensions={0} | all-to-all | bytes 2359296 | tf_op jit(solution)/shard_map/all_to_all | solution.py:36
  412.2 18.6 %all_to_all.104 = bf16[64,2,1152]{2,1,0:T(2,128)(2,1)S(1)} all-to-all(bf16[64,2,1152]{2,1,0:T(2,128)(2,1)S(1)} %reshape.505), channel_id=1, replica_groups=mesh['zh'=2,'zl'=4,'y'=4,'xl'=2,'xh'=2,'c'=2] {'zh','zl','y','xl'}, dimensions={0} | all-to-all | bytes 589824 | tf_op jit(solution)/shard_map/all_to_all | solution.py:36
  (200 shorter events, 131.8 us)
Async XLA Ops:
  6.5 57.3 %copy-start = (bf16[1,128,1152]{2,1,0:T(8,128)(2,1)S(1)}, bf16[1,128,1152]{2,1,0:T(8,128)(2,1)}, u32[]{:S(2)}) copy-start(bf16[1,128,1152]{2,1,0:T(8,128)(2,1)} %param.7) | copy-start | bytes 884740
  6.5 353.1 %all-gather.3.cloned.1.call-start = ((), (), s32[]{:S(2)}) async-start(), calls=%async_computation.19 | async-start | bytes 16422912 | tf_op jit(solution)/shard_map/all_gather | solution.py:145
  45.2 18.7 %copy-start.2 = (bf16[1152,1152]{1,0:T(8,128)(2,1)S(1)}, bf16[1152,1152]{1,0:T(8,128)(2,1)}, u32[]{:S(2)}) copy-start(bf16[1152,1152]{1,0:T(8,128)(2,1)} %constant.37.clone) | copy-start | bytes 7962628
  50.1 29.7 %all-to-all-start.2 = ((bf16[16,18,576]{2,1,0:T(8,128)(2,1)}), bf16[16,18,576]{2,1,0:T(8,128)(2,1)}, u32[]{:S(2)}, u32[]{:S(2)}) async-start(bf16[16,18,576]{2,1,0:T(8,128)(2,1)} %bitcast.10), calls=%async_computation.2 | async-start | bytes 983040 | tf_op jit(solution)/shard_map/all_to_all | solution.py:36
  80.9 14.2 %all-to-all-start = ((bf16[4,128,1152]{2,1,0:T(8,128)(2,1)}), bf16[4,128,1152]{2,1,0:T(8,128)(2,1)S(1)}, u32[]{:S(2)}, u32[]{:S(2)}) async-start(bf16[4,128,1152]{2,1,0:T(8,128)(2,1)} %broadcast_in_dim.26), calls=%async_computation | async-start | bytes 2359296 | tf_op jit(solution)/shard_map/all_to_all | solution.py:36
  95.4 5.8 %copy-start.6 = (bf16[288,576]{1,0:T(8,128)(2,1)S(1)}, bf16[288,576]{1,0:T(8,128)(2,1)}, u32[]{:S(2)}) copy-start(bf16[288,576]{1,0:T(8,128)(2,1)} %broadcast_in_dim.29) | copy-start | bytes 995332
  101.2 6.0 %copy-start.9 = (bf16[18,1152]{1,0:T(8,128)(2,1)S(1)}, bf16[18,1152]{1,0:T(8,128)(2,1)}, u32[]{:S(2)}) copy-start(bf16[18,1152]{1,0:T(8,128)(2,1)} %get-tuple-element.10) | copy-start | bytes 124420
  101.2 6.1 %copy-start.10 = (bf16[18,1152]{1,0:T(8,128)(2,1)S(1)}, bf16[18,1152]{1,0:T(8,128)(2,1)}, u32[]{:S(2)}) copy-start(bf16[18,1152]{1,0:T(8,128)(2,1)} %get-tuple-element.8) | copy-start | bytes 124420
  102.4 41.0 %all-to-all-start.3 = ((bf16[4,288,576]{2,1,0:T(8,128)(2,1)}), bf16[4,288,576]{2,1,0:T(8,128)(2,1)}, u32[]{:S(2)}, u32[]{:S(2)}) async-start(bf16[4,288,576]{2,1,0:T(8,128)(2,1)} %broadcast_in_dim.30), calls=%async_computation.3 | async-start | bytes 2949120 | tf_op jit(solution)/shard_map/all_to_all | solution.py:36
  167.8 39.3 %all-to-all-start.8 = ((bf16[16,18,1152]{2,1,0:T(8,128)(2,1)}), bf16[16,18,1152]{2,1,0:T(8,128)(2,1)}, u32[]{:S(2)}, u32[]{:S(2)}) async-start(bf16[16,18,1152]{2,1,0:T(8,128)(2,1)} %bitcast.176), calls=%async_computation.8 | async-start | bytes 1769472 | tf_op jit(solution)/shard_map/all_to_all | solution.py:36
  207.1 18.8 %all-to-all-start.5 = ((bf16[4,128,1152]{2,1,0:T(8,128)(2,1)}), bf16[4,128,1152]{2,1,0:T(8,128)(2,1)S(1)}, u32[]{:S(2)}, u32[]{:S(2)}) async-start(bf16[4,128,1152]{2,1,0:T(8,128)(2,1)} %bitcast.174), calls=%async_computation.5 | async-start | bytes 2359296 | tf_op jit(solution)/shard_map/all_to_all | solution.py:36
  227.8 35.8 %all-to-all-start.9 = ((bf16[4,288,1152]{2,1,0:T(8,128)(2,1)}), bf16[4,288,1152]{2,1,0:T(8,128)(2,1)S(1)}, u32[]{:S(2)}, u32[]{:S(2)}) async-start(bf16[4,288,1152]{2,1,0:T(8,128)(2,1)} %broadcast_in_dim.35), calls=%async_computation.9 | async-start | bytes 5308416 | tf_op jit(solution)/shard_map/all_to_all | solution.py:36
  264.7 20.3 %all-to-all-start.6 = ((bf16[4,128,1152]{2,1,0:T(8,128)(2,1)}), bf16[4,128,1152]{2,1,0:T(8,128)(2,1)}, u32[]{:S(2)}, u32[]{:S(2)}) async-start(bf16[4,128,1152]{2,1,0:T(8,128)(2,1)} %broadcast_in_dim.31), calls=%async_computation.6 | async-start | bytes 2359296 | tf_op jit(solution)/shard_map/all_to_all | solution.py:36
  309.7 7.1 %copy-start.16 = (f32[1,1,16,2,36]{4,3,2,1,0:T(2,128)S(1)}, f32[1,1,16,2,36]{4,3,2,1,0:T(2,128)}, u32[]{:S(2)}) copy-start(f32[1,1,16,2,36]{4,3,2,1,0:T(2,128)} %get-tuple-element.32) | copy-start | bytes 13828
  311.5 20.3 %all-to-all-start.11 = ((bf16[4,128,1152]{2,1,0:T(8,128)(2,1)}), bf16[4,128,1152]{2,1,0:T(8,128)(2,1)S(1)}, u32[]{:S(2)}, u32[]{:S(2)}) async-start(bf16[4,128,1152]{2,1,0:T(8,128)(2,1)} %bitcast.175), calls=%async_computation.11 | async-start | bytes 2359296 | tf_op jit(solution)/shard_map/all_to_all | solution.py:36
  316.8 23.6 %copy-start.15 = (f32[1,1,16,2,36]{4,3,2,1,0:T(2,128)S(1)}, f32[1,1,16,2,36]{4,3,2,1,0:T(2,128)}, u32[]{:S(2)}) copy-start(f32[1,1,16,2,36]{4,3,2,1,0:T(2,128)} %get-tuple-element.28) | copy-start | bytes 13828
  316.8 23.8 %copy-start.14 = (f32[1,1,16,2,36]{4,3,2,1,0:T(2,128)S(1)}, f32[1,1,16,2,36]{4,3,2,1,0:T(2,128)}, u32[]{:S(2)}) copy-start(f32[1,1,16,2,36]{4,3,2,1,0:T(2,128)} %get-tuple-element.27) | copy-start | bytes 13828
  316.8 23.9 %copy-start.13 = (f32[1,1,16,2,36]{4,3,2,1,0:T(2,128)S(1)}, f32[1,1,16,2,36]{4,3,2,1,0:T(2,128)}, u32[]{:S(2)}) copy-start(f32[1,1,16,2,36]{4,3,2,1,0:T(2,128)} %get-tuple-element.29) | copy-start | bytes 13828
  316.8 24.0 %copy-start.12 = (f32[1,1,16,2,36]{4,3,2,1,0:T(2,128)S(1)}, f32[1,1,16,2,36]{4,3,2,1,0:T(2,128)}, u32[]{:S(2)}) copy-start(f32[1,1,16,2,36]{4,3,2,1,0:T(2,128)} %get-tuple-element.26) | copy-start | bytes 13828
  316.8 24.1 %copy-start.11 = (f32[1,1,16,2,36]{4,3,2,1,0:T(2,128)S(1)}, f32[1,1,16,2,36]{4,3,2,1,0:T(2,128)}, u32[]{:S(2)}) copy-start(f32[1,1,16,2,36]{4,3,2,1,0:T(2,128)} %get-tuple-element.25) | copy-start | bytes 13828
  332.9 20.7 %all-to-all-start.12 = ((bf16[64,2,1152]{2,1,0:T(2,128)(2,1)}), bf16[64,2,1152]{2,1,0:T(2,128)(2,1)S(1)}, u32[]{:S(2)}, u32[]{:S(2)}) async-start(bf16[64,2,1152]{2,1,0:T(2,128)(2,1)} %reshape.483), calls=%async_computation.12 | async-start | bytes 589824 | tf_op jit(solution)/shard_map/all_to_all | solution.py:36
  400.1 8.4 %copy-start.3 = (bf16[1152,1152]{1,0:T(8,128)(2,1)S(1)}, bf16[1152,1152]{1,0:T(8,128)(2,1)}, u32[]{:S(2)}) copy-start(bf16[1152,1152]{1,0:T(8,128)(2,1)} %constant.37.clone) | copy-start | bytes 7962628
  400.1 8.4 %copy-start.20 = (f32[1152]{0:T(1024)S(1)}, f32[1152]{0:T(1024)}, u32[]{:S(2)}) copy-start(f32[1152]{0:T(1024)} %mul.236) | copy-start | bytes 13828
  408.5 23.2 %copy-start.1 = (bf16[1,128,1152]{2,1,0:T(8,128)(2,1)S(1)}, bf16[1,128,1152]{2,1,0:T(8,128)(2,1)}, u32[]{:S(2)}) copy-start(bf16[1,128,1152]{2,1,0:T(8,128)(2,1)} %param.7) | copy-start | bytes 884740
  (11 other events, 29.6 us)
Sparse Core Ops, SparseCore 0:
  47.4 174.8 all-gather.2
